TPU v7x, 512 devices: a whole 4x8x8 slice. The times are simulated.
512 devices in a mesh: seq: 32 (over z, x_hi, core), tok: 16 (over x_lo, y).
Axes of the slice: x: 4 (x_hi: 2, x_lo: 2; x = x_hi * 2 + x_lo), y: 8, z: 8, core: 2. Of those that a mesh axis runs over, the one named last changes fastest.
Arguments:
- cotangent: bfloat16 [32, 2048, 2048], P('seq', 'tok'), may hold values from -6 to 6
- gate_values: bfloat16 [32, 2048, 2048], P('seq', 'tok'), may hold values from -6 to 6
- conv_input: bfloat16 [32, 2048, 2048], P('seq', 'tok'), may hold values from -6 to 6
- filter_taps: float32 [2048, 2048], P('tok', 'seq'), may hold values from -0.125 to 0.125
- first_moment: float32 [2048, 2048], P('tok', 'seq'), may hold values from -12 to 12
- second_moment: float32 [2048, 2048], P('tok', 'seq'), may hold values from 0.1 to 2
Outputs:
- grad_input: bfloat16 [32, 2048, 2048], P('seq', 'tok')
- new_taps: float32 [2048, 2048], P('tok', 'seq')
- new_first: float32 [2048, 2048], P('tok', 'seq')
- new_second: float32 [2048, 2048], P('tok', 'seq')
All inputs are finite; a program needn't handle non-finite values.
Results may differ from a plain program's by a relative error of at most 0.0049.
Values may be sent and summed in bfloat16 or wider, within the bound.
A program may use at most 64 MiB of HBM per device.

v0:
```python
import jax
import jax.numpy as jnp
import numpy as np
from jax import lax
from jax.experimental import pallas as pl
from jax.experimental.pallas import tpu as pltpu
from jax.sharding import PartitionSpec as P

beta_one = 0.9
beta_two = 0.999
learn_rate = 0.05
adam_step = 10
adam_eps = 1e-08

MESH = pl.DeviceIdType.MESH
LANES = 128
TOK = 16
OWNERS = 16
LAGS = 64
BLOCK = 256
PAIRS = 4
FREQS = 256


def transform_matrices():
    order = np.concatenate([np.arange(0, FREQS, 2), np.arange(1, FREQS, 2)])
    angle = 2.0 * np.pi * np.outer(order + 0.5, np.arange(BLOCK)) / (2 * BLOCK)
    ahead = np.concatenate([np.cos(angle), -np.sin(angle)])
    back = ahead.T / FREQS

    def split(matrix):
        high = matrix.astype(jnp.bfloat16)
        low = (matrix - high.astype(np.float64)).astype(jnp.bfloat16)
        return np.stack([high, low])

    return split(ahead), split(back)


def forward(source_ref, spec_ref, ahead_ref):
    def pair(p, carry):
        row = pl.multiple_of(p * (2 * BLOCK), 2 * BLOCK)
        both = jnp.concatenate(
            [source_ref[pl.ds(row, BLOCK), :], source_ref[pl.ds(row + BLOCK, BLOCK), :]], axis=1
        )
        spec_ref[p] = jnp.dot(
            ahead_ref[0], both, preferred_element_type=jnp.float32
        ) + jnp.dot(ahead_ref[1], both, preferred_element_type=jnp.float32)
        return carry

    lax.fori_loop(0, PAIRS, pair, 0)


def correlate(left_ref, right_ref, out_ref):
    blocks = 2 * PAIRS

    def tiles(sign, start):
        def tile(step, carry):
            row = pl.multiple_of(start + step * 8, 8)
            real, imag = pl.ds(row, 8), pl.ds(row + FREQS, 8)

            def get(ref, j, rows):
                return ref[j // 2, rows, (j % 2) * LANES : (j % 2 + 1) * LANES]

            left_re = [get(left_ref, j, real) for j in range(blocks)]
            left_im = [get(left_ref, j, imag) for j in range(blocks)]
            right_re = [get(right_ref, j, real) for j in range(blocks)]
            right_im = [get(right_ref, j, imag) for j in range(blocks)]
            win_re, win_im = [right_re[0]], [right_im[0]]
            for d in range(1, blocks):
                if sign > 0:
                    win_re.append(right_re[d] - right_im[d - 1])
                    win_im.append(right_im[d] + right_re[d - 1])
                else:
                    win_re.append(right_re[d] + right_im[d - 1])
                    win_im.append(right_im[d] - right_re[d - 1])
            for i in range(blocks):
                out_re = left_re[i] * win_re[0] + left_im[i] * win_im[0]
                out_im = left_im[i] * win_re[0] - left_re[i] * win_im[0]
                for d in range(1, blocks - i):
                    out_re += left_re[i + d] * win_re[d] + left_im[i + d] * win_im[d]
                    out_im += left_im[i + d] * win_re[d] - left_re[i + d] * win_im[d]
                lanes = slice((i % 2) * LANES, (i % 2 + 1) * LANES)
                out_ref[i // 2, real, lanes] = out_re
                out_ref[i // 2, imag, lanes] = out_im
            return carry

        lax.fori_loop(0, FREQS // 16, tile, 0)

    tiles(1, 0)
    tiles(-1, FREQS // 2)


def backward(spec_ref, back_ref, p):
    both = spec_ref[p].astype(jnp.bfloat16)
    return jnp.dot(back_ref[0], both, preferred_element_type=jnp.float32) + jnp.dot(
        back_ref[1], both, preferred_element_type=jnp.float32
    )


def kernel(
    cot_hbm,
    gate_hbm,
    input_hbm,
    taps_ref,
    ahead_hbm,
    back_hbm,
    grad_out,
    sums_out,
    cot,
    gate,
    ahead,
    back,
    scaled_out,
    input_out,
    scaled_in,
    input_in,
    taps_in,
    grad_buf,
    pair_out,
    pair_in,
    owner_out,
    owner_in,
    spec_scaled,
    spec_right,
    spec_prod,
    sums,
    load_sem,
    input_sem,
    local_sem,
    scaled_send,
    scaled_recv,
    input_send,
    input_recv,
    taps_send,
    taps_recv,
    grad_send,
    grad_recv,
    owner_send,
    owner_recv,
    pair_send,
    pair_recv,
):
    seq, tok = lax.axis_index("seq"), lax.axis_index("tok")
    core, owner = seq % 2, seq // 2
    sibling = (seq + 1 - 2 * core, tok)

    def tok_peer(o):
        return lax.rem(tok + o, TOK)

    def owner_peer(o):
        return lax.rem(owner + o, OWNERS)

    loads = [
        pltpu.make_async_copy(src, dst, load_sem.at[i])
        for i, (src, dst) in enumerate(
            [(cot_hbm.at[0], cot), (gate_hbm.at[0], gate), (ahead_hbm, ahead), (back_hbm, back)]
        )
    ]
    for load in loads:
        load.start()

    def input_load(c):
        lanes = pl.ds(pl.multiple_of(c * LANES, LANES), LANES)
        return pltpu.make_async_copy(
            input_hbm.at[0, :, lanes], input_out.at[c], input_sem.at[c]
        )

    barrier = pltpu.get_barrier_semaphore()

    def greet(o, carry):
        pl.semaphore_signal(barrier, inc=1, device_id=(seq, tok_peer(o)), device_id_type=MESH)
        pl.semaphore_signal(
            barrier, inc=1, device_id=(owner_peer(o) * 2 + core, tok), device_id_type=MESH
        )
        return carry

    lax.fori_loop(1, TOK, greet, 0)
    pl.semaphore_signal(barrier, inc=1, device_id=sibling, device_id_type=MESH)

    def start_input_load(c, carry):
        input_load(c).start()
        return carry

    lax.fori_loop(0, TOK, start_input_load, 0)
    taps_in[owner, core] = jnp.transpose(taps_ref[...]).astype(jnp.bfloat16)
    loads[0].wait()
    loads[1].wait()

    def scale(c, carry):
        lanes = pl.ds(pl.multiple_of(c * LANES, LANES), LANES)
        scaled_out[c] = (
            cot[:, lanes].astype(jnp.float32) * gate[:, lanes].astype(jnp.float32)
        ).astype(jnp.bfloat16)
        return carry

    lax.fori_loop(0, TOK, scale, 0)
    my_rows = pl.ds(pl.multiple_of(tok * LANES, LANES), LANES)
    scaled_in[my_rows, :] = scaled_out[tok]

    def wait_input_load(c, carry):
        input_load(c).wait()
        return carry

    lax.fori_loop(0, TOK, wait_input_load, 0)
    input_in[my_rows, :] = input_out[tok]
    loads[2].wait()
    loads[3].wait()
    pl.semaphore_wait(barrier, 2 * (TOK - 1) + 1)

    def scaled_copy(to, frm):
        rows = pl.ds(pl.multiple_of(frm * LANES, LANES), LANES)
        return pltpu.make_async_remote_copy(
            src_ref=scaled_out.at[to],
            dst_ref=scaled_in.at[rows, :],
            send_sem=scaled_send.at[to],
            recv_sem=scaled_recv.at[frm],
            device_id=(seq, to),
            device_id_type=MESH,
        )

    def input_copy(to, frm):
        rows = pl.ds(pl.multiple_of(frm * LANES, LANES), LANES)
        return pltpu.make_async_remote_copy(
            src_ref=input_out.at[to],
            dst_ref=input_in.at[rows, :],
            send_sem=input_send.at[to],
            recv_sem=input_recv.at[frm],
            device_id=(seq, to),
            device_id_type=MESH,
        )

    def taps_copy(to, frm):
        return pltpu.make_async_remote_copy(
            src_ref=taps_in.at[frm, core],
            dst_ref=taps_in.at[frm, core],
            send_sem=taps_send.at[to],
            recv_sem=taps_recv.at[frm],
            device_id=(to * 2 + core, tok),
            device_id_type=MESH,
        )

    def grad_copy(to, frm):
        return pltpu.make_async_remote_copy(
            src_ref=grad_buf.at[to],
            dst_ref=grad_out.at[frm],
            send_sem=grad_send.at[to],
            recv_sem=grad_recv.at[frm],
            device_id=(seq, to),
            device_id_type=MESH,
        )

    def owner_copy(to, frm):
        return pltpu.make_async_remote_copy(
            src_ref=owner_out.at[to],
            dst_ref=owner_in.at[frm],
            send_sem=owner_send.at[to],
            recv_sem=owner_recv.at[frm],
            device_id=(to * 2 + core, tok),
            device_id_type=MESH,
        )

    def send_first(o, carry):
        scaled_copy(tok_peer(o), tok).start()
        taps_copy(owner_peer(o), owner).start()
        return carry

    lax.fori_loop(1, TOK, send_first, 0)

    def send_input(o, carry):
        input_copy(tok_peer(o), tok).start()
        return carry

    lax.fori_loop(1, TOK, send_input, 0)

    def taps_arrive(o, carry):
        taps_copy(owner, owner_peer(o)).wait_recv()
        return carry

    lax.fori_loop(1, OWNERS, taps_arrive, 0)

    def taps_pair(which):
        return pltpu.make_async_remote_copy(
            src_ref=taps_in.at[:, which],
            dst_ref=taps_in.at[:, which],
            send_sem=pair_send.at[0],
            recv_sem=pair_recv.at[0],
            device_id=sibling,
            device_id_type=MESH,
        )

    taps_pair(core).start()

    def scaled_arrive(o, carry):
        scaled_copy(tok, tok_peer(o)).wait_recv()
        return carry

    lax.fori_loop(1, TOK, scaled_arrive, 0)
    forward(scaled_in, spec_scaled, ahead)
    taps_pair(1 - core).wait_recv()

    def taps_forward(p, carry):
        both = jnp.concatenate(
            [
                taps_in[pl.ds(p * 4, 2)].reshape(BLOCK, LANES),
                taps_in[pl.ds(p * 4 + 2, 2)].reshape(BLOCK, LANES),
            ],
            axis=1,
        )
        spec_right[p] = jnp.dot(
            ahead[0], both, preferred_element_type=jnp.float32
        ) + jnp.dot(ahead[1], both, preferred_element_type=jnp.float32)
        return carry

    lax.fori_loop(0, PAIRS, taps_forward, 0)
    correlate(spec_scaled, spec_right, spec_prod)

    def grad_back(p, carry):
        both = backward(spec_prod, back, p).astype(jnp.bfloat16)
        for half in range(2):
            for part in range(2):
                grad_buf[p * 4 + half * 2 + part] = both[
                    part * LANES : (part + 1) * LANES, half * LANES : (half + 1) * LANES
                ]
        return carry

    lax.fori_loop(0, PAIRS, grad_back, 0)

    def send_grad(o, carry):
        grad_copy(tok_peer(o), tok).start()
        return carry

    lax.fori_loop(1, TOK, send_grad, 0)
    own_grad = pltpu.make_async_copy(grad_buf.at[tok], grad_out.at[tok], local_sem)
    own_grad.start()

    def input_arrive(o, carry):
        input_copy(tok, tok_peer(o)).wait_recv()
        return carry

    lax.fori_loop(1, TOK, input_arrive, 0)
    forward(input_in, spec_right, ahead)
    correlate(spec_scaled, spec_right, spec_prod)

    def sums_back(p, carry):
        both = backward(spec_prod, back, p)
        for half in range(2):
            sums[pl.ds(p * 4 + half * 2, 2)] = both[
                :, half * LANES : (half + 1) * LANES
            ].reshape(2, 2, LAGS, LANES)
        return carry

    lax.fori_loop(0, PAIRS, sums_back, 0)

    def cut(q, carry):
        pair_out[q] = sums[q, 1 - core].astype(jnp.bfloat16)
        return carry

    lax.fori_loop(0, OWNERS, cut, 0)
    pair_copy = pltpu.make_async_remote_copy(
        src_ref=pair_out,
        dst_ref=pair_in,
        send_sem=pair_send.at[1],
        recv_sem=pair_recv.at[1],
        device_id=sibling,
        device_id_type=MESH,
    )
    pair_copy.start()
    pair_copy.wait_recv()

    def join(q, carry):
        owner_out[q] = (sums[q, core] + pair_in[q].astype(jnp.float32)).astype(jnp.bfloat16)
        return carry

    lax.fori_loop(0, OWNERS, join, 0)

    def send_owner(o, carry):
        owner_copy(owner_peer(o), owner).start()
        return carry

    lax.fori_loop(1, OWNERS, send_owner, 0)
    owner_in[owner] = owner_out[owner]

    def owner_arrive(o, carry):
        owner_copy(owner, owner_peer(o)).wait_recv()
        return carry

    lax.fori_loop(1, OWNERS, owner_arrive, 0)
    total = owner_in[0].astype(jnp.float32)
    for q in range(1, OWNERS):
        total += owner_in[q].astype(jnp.float32)
    sums_out[...] = jnp.transpose(total)

    def finish(o, carry):
        scaled_copy(tok_peer(o), tok).wait_send()
        input_copy(tok_peer(o), tok).wait_send()
        taps_copy(owner_peer(o), owner).wait_send()
        grad_copy(tok_peer(o), tok).wait_send()
        owner_copy(owner_peer(o), owner).wait_send()
        grad_copy(tok, tok_peer(o)).wait_recv()
        return carry

    lax.fori_loop(1, TOK, finish, 0)
    taps_pair(core).wait_send()
    pair_copy.wait_send()
    own_grad.wait()


def shards(cotangent, gate_values, conv_input, filter_taps, first_moment, second_moment):
    ahead, back = transform_matrices()
    bf16, f32 = jnp.bfloat16, jnp.float32
    hbm = pl.BlockSpec(memory_space=pl.ANY)
    vmem = pl.BlockSpec(memory_space=pltpu.VMEM)
    width = TOK * LANES
    tokens = 2 * PAIRS * BLOCK
    spec = pltpu.VMEM((PAIRS, 2 * FREQS, 2 * LANES), f32)
    dma = pltpu.SemaphoreType.DMA
    blocks, summed = pl.pallas_call(
        kernel,
        out_shape=(
            jax.ShapeDtypeStruct((TOK, LANES, LANES), bf16),
            jax.ShapeDtypeStruct((LANES, LAGS), f32),
        ),
        in_specs=[hbm, hbm, hbm, vmem, hbm, hbm],
        out_specs=(hbm, vmem),
        scratch_shapes=[
            pltpu.VMEM((LANES, width), bf16),
            pltpu.VMEM((LANES, width), bf16),
            pltpu.VMEM(ahead.shape, bf16),
            pltpu.VMEM(back.shape, bf16),
            pltpu.VMEM((TOK, LANES, LANES), bf16),
            pltpu.VMEM((TOK, LANES, LANES), bf16),
            pltpu.VMEM((tokens, LANES), bf16),
            pltpu.VMEM((tokens, LANES), bf16),
            pltpu.VMEM((OWNERS, 2, LAGS, LANES), bf16),
            pltpu.VMEM((TOK, LANES, LANES), bf16),
            pltpu.VMEM((OWNERS, LAGS, LANES), bf16),
            pltpu.VMEM((OWNERS, LAGS, LANES), bf16),
            pltpu.VMEM((OWNERS, LAGS, LANES), bf16),
            pltpu.VMEM((OWNERS, LAGS, LANES), bf16),
            spec,
            spec,
            spec,
            pltpu.VMEM((OWNERS, 2, LAGS, LANES), f32),
            dma((4,)),
            dma((TOK,)),
            dma,
            dma((TOK,)),
            dma((TOK,)),
            dma((TOK,)),
            dma((TOK,)),
            dma((OWNERS,)),
            dma((OWNERS,)),
            dma((TOK,)),
            dma((TOK,)),
            dma((OWNERS,)),
            dma((OWNERS,)),
            dma((2,)),
            dma((2,)),
        ],
        compiler_params=pltpu.CompilerParams(
            collective_id=0, has_side_effects=True, vmem_limit_bytes=48 << 20
        ),
        name="gated_conv_backward",
    )(cotangent, gate_values, conv_input, filter_taps, ahead, back)
    grad_input = jnp.moveaxis(blocks, 0, 1).reshape(LANES, width)
    taps_grad = summed / lax.axis_size("seq")
    new_first = beta_one * first_moment + (1.0 - beta_one) * taps_grad
    new_second = beta_two * second_moment + (1.0 - beta_two) * taps_grad * taps_grad
    first_hat = new_first / (1.0 - beta_one**adam_step)
    second_hat = new_second / (1.0 - beta_two**adam_step)
    new_taps = filter_taps - learn_rate * first_hat / (jnp.sqrt(second_hat) + adam_eps)
    return (grad_input[None], new_taps, new_first, new_second)


def solution(mesh):
    placed = (
        P("seq", "tok", None),
        P("seq", "tok", None),
        P("seq", "tok", None),
        P("tok", "seq"),
        P("tok", "seq"),
        P("tok", "seq"),
    )
    return jax.shard_map(
        shards,
        mesh=mesh,
        in_specs=placed,
        out_specs=(P("seq", "tok", None), P("tok", "seq"), P("tok", "seq"), P("tok", "seq")),
        check_vma=False,
    )
```

profile of v0, /device:TPU:1, one launch (start us, length us, event | category | flops | bytes accessed | tf_op | source)
XLA Modules:
  0.0 69.2 jit_solution(5202443311105566376)
XLA Ops:
  0.6 0.8 %copy.19.taps_ref = f32[128,64]{1,0:T(8,128)S(1)} copy(f32[128,64]{0,1:T(8,128)} %param.11) | data formatting | bytes 65536 | tf_op args[3]
  1.5 0.0 copy-start
  1.5 1.0 %copy-done = bf16[1,128,2048]{2,1,0:T(8,128)(2,1)S(1)} copy-done((bf16[1,128,2048]{2,1,0:T(8,128)(2,1)S(1)}, bf16[1,128,2048]{2,1,0:T(8,128)(2,1)}, u32[]{:S(2)}) %copy-start) | copy-done | bytes 524312
  2.5 0.0 copy-start.1
  2.5 1.0 %copy-done.1 = bf16[1,128,2048]{2,1,0:T(8,128)(2,1)S(1)} copy-done((bf16[1,128,2048]{2,1,0:T(8,128)(2,1)S(1)}, bf16[1,128,2048]{2,1,0:T(8,128)(2,1)}, u32[]{:S(2)}) %copy-start.1) | copy-done | bytes 524312
  3.6 0.0 copy-start.2
  3.6 1.0 %copy-done.2 = bf16[1,128,2048]{2,1,0:T(8,128)(2,1)S(1)} copy-done((bf16[1,128,2048]{2,1,0:T(8,128)(2,1)S(1)}, bf16[1,128,2048]{2,1,0:T(8,128)(2,1)}, u32[]{:S(2)}) %copy-start.2) | copy-done | bytes 524312
  4.6 0.0 copy-start.3
  4.6 1.0 %copy-done.3 = bf16[2,512,256]{2,1,0:T(8,128)(2,1)S(1)} copy-done((bf16[2,512,256]{2,1,0:T(8,128)(2,1)S(1)}, bf16[2,512,256]{2,1,0:T(8,128)(2,1)}, u32[]{:S(2)}) %copy-start.3) | copy-done | bytes 524312
  5.7 0.0 copy-start.4
  5.7 1.0 %copy-done.4 = bf16[2,256,512]{2,1,0:T(8,128)(2,1)S(1)} copy-done((bf16[2,256,512]{2,1,0:T(8,128)(2,1)S(1)}, bf16[2,256,512]{2,1,0:T(8,128)(2,1)}, u32[]{:S(2)}) %copy-start.4) | copy-done | bytes 524312
  6.7 0.0 copy-start.5
  6.7 58.1 %gated_conv_backward.1 = (bf16[16,128,128]{2,1,0:T(8,128)(2,1)S(1)}, f32[128,64]{1,0:T(8,128)S(1)}) custom-call(bf16[1,128,2048]{2,1,0:T(8,128)(2,1)S(1)} %copy-done, bf16[1,128,2048]{2,1,0:T(8,128)(2,1)S(1)} %copy-done.1, bf16[1,128,2048]{2,1,0:T(8,128)(2,1)S(1)} %copy-done.2, f32[128,64]{1,0:T(8,128)S(1)} %copy.19.taps_ref, ...), custom_call_target="tpu_custom_call" | custom-call | tf_op jit(solution)/shard_map/gated_conv_backward/pallas_call | solution.py:417
  64.8 0.0 copy-done.5
  64.8 0.0 copy-start.6
  64.9 0.1 copy.21
  65.0 0.7 copy-done.6
  65.6 0.1 copy.22
  65.7 0.1 divide_subtract_fusion
  65.8 0.7 %copy.25 = f32[128,64]{0,1:T(8,128)} copy(f32[128,64]{1,0:T(8,128)S(1)} %get-tuple-element.16) | data formatting | bytes 65536
  66.5 0.7 %copy.26 = f32[128,64]{0,1:T(8,128)} copy(f32[128,64]{1,0:T(8,128)S(1)} %get-tuple-element.17) | data formatting | bytes 65536
  67.2 0.7 %copy.27 = f32[128,64]{0,1:T(8,128)} copy(f32[128,64]{1,0:T(8,128)S(1)} %get-tuple-element.18) | data formatting | bytes 65536
  67.9 0.3 copy.20
  68.1 1.0 %copy.24 = bf16[1,128,2048]{2,1,0:T(8,128)(2,1)} copy(bf16[1,128,2048]{1,2,0:T(8,128)(2,1)S(1)} %bitcast.3) | data formatting | bytes 1048576
Async XLA Ops:
  1.5 1.0 %copy-start = (bf16[1,128,2048]{2,1,0:T(8,128)(2,1)S(1)}, bf16[1,128,2048]{2,1,0:T(8,128)(2,1)}, u32[]{:S(2)}) copy-start(bf16[1,128,2048]{2,1,0:T(8,128)(2,1)} %cot_hbm.1) | copy-start | bytes 1572868
  2.5 1.0 %copy-start.1 = (bf16[1,128,2048]{2,1,0:T(8,128)(2,1)S(1)}, bf16[1,128,2048]{2,1,0:T(8,128)(2,1)}, u32[]{:S(2)}) copy-start(bf16[1,128,2048]{2,1,0:T(8,128)(2,1)} %gate_hbm.1) | copy-start | bytes 1572868
  3.6 1.0 %copy-start.2 = (bf16[1,128,2048]{2,1,0:T(8,128)(2,1)S(1)}, bf16[1,128,2048]{2,1,0:T(8,128)(2,1)}, u32[]{:S(2)}) copy-start(bf16[1,128,2048]{2,1,0:T(8,128)(2,1)} %input_hbm.1) | copy-start | bytes 1572868
  4.6 1.0 %copy-start.3 = (bf16[2,512,256]{2,1,0:T(8,128)(2,1)S(1)}, bf16[2,512,256]{2,1,0:T(8,128)(2,1)}, u32[]{:S(2)}) copy-start(bf16[2,512,256]{2,1,0:T(8,128)(2,1)} %constant.27.clone.ahead_hbm) | copy-start | bytes 1572868
  5.7 1.0 %copy-start.4 = (bf16[2,256,512]{2,1,0:T(8,128)(2,1)S(1)}, bf16[2,256,512]{2,1,0:T(8,128)(2,1)}, u32[]{:S(2)}) copy-start(bf16[2,256,512]{2,1,0:T(8,128)(2,1)} %constant.28.clone.back_hbm) | copy-start | bytes 1572868
  6.7 58.1 %copy-start.5 = (f32[128,64]{0,1:T(8,128)S(1)}, f32[128,64]{0,1:T(8,128)}, u32[]{:S(2)}) copy-start(f32[128,64]{0,1:T(8,128)} %param.12) | copy-start | bytes 98308
  64.8 0.8 %copy-start.6 = (f32[128,64]{0,1:T(8,128)S(1)}, f32[128,64]{0,1:T(8,128)}, u32[]{:S(2)}) copy-start(f32[128,64]{0,1:T(8,128)} %param.13) | copy-start | bytes 98308
where the time goes:
time: 69.7 us; the launch traced here: 69.2 us
  Pallas kernels  58.1 us (83%)
  local copies, waits for them, and re-layouts  10.3 us (15%)
    pallas_call x1, Pallas kernels, shards(): pl.pallas_call(kernel, out_shape=(jax.ShapeDtypeStruct((TOK, LANES, LANES...  58.1 us
    unnamed x21, local copies, waits for them, and re-layouts  10 us

commit v1 on v0

--- a/solution.py
+++ b/solution.py
@@ -19,6 +19,7 @@
 LAGS = 64
 BLOCK = 256
 PAIRS = 4
+PIECES = 16
 FREQS = 256
 
 
@@ -182,7 +183,7 @@
         return carry
 
     lax.fori_loop(0, TOK, start_input_load, 0)
-    taps_in[owner, core] = jnp.transpose(taps_ref[...]).astype(jnp.bfloat16)
+    taps_in[owner, core] = taps_ref[...].astype(jnp.bfloat16)
     loads[0].wait()
     loads[1].wait()
 
@@ -240,9 +241,10 @@
         )
 
     def grad_copy(to, frm):
+        lanes = pl.ds(pl.multiple_of(frm * LANES, LANES), LANES)
         return pltpu.make_async_remote_copy(
             src_ref=grad_buf.at[to],
-            dst_ref=grad_out.at[frm],
+            dst_ref=grad_out.at[0, :, lanes],
             send_sem=grad_send.at[to],
             recv_sem=grad_recv.at[frm],
             device_id=(seq, to),
@@ -330,7 +332,8 @@
         return carry
 
     lax.fori_loop(1, TOK, send_grad, 0)
-    own_grad = pltpu.make_async_copy(grad_buf.at[tok], grad_out.at[tok], local_sem)
+    my_lanes = pl.ds(pl.multiple_of(tok * LANES, LANES), LANES)
+    own_grad = pltpu.make_async_copy(grad_buf.at[tok], grad_out.at[0, :, my_lanes], local_sem)
     own_grad.start()
 
     def input_arrive(o, carry):
@@ -388,7 +391,7 @@
     total = owner_in[0].astype(jnp.float32)
     for q in range(1, OWNERS):
         total += owner_in[q].astype(jnp.float32)
-    sums_out[...] = jnp.transpose(total)
+    sums_out[...] = total
 
     def finish(o, carry):
         scaled_copy(tok_peer(o), tok).wait_send()
@@ -403,6 +406,32 @@
     taps_pair(core).wait_send()
     pair_copy.wait_send()
     own_grad.wait()
+
+
+def update_kernel(
+    grad_ref, sums_ref, taps_ref, first_ref, second_ref, grad_out, taps_out, first_out, second_out, held, in_sem, out_sem
+):
+    rows = LANES // PIECES
+    arrive, leave = [], []
+    for i in range(PIECES):
+        piece = pl.ds(i * rows, rows)
+        arrive.append(pltpu.make_async_copy(grad_ref.at[0, piece], held.at[piece], in_sem.at[i]))
+        leave.append(pltpu.make_async_copy(held.at[piece], grad_out.at[0, piece], out_sem.at[i]))
+    for copy in arrive:
+        copy.start()
+    for copy, onward in zip(arrive, leave):
+        copy.wait()
+        onward.start()
+    taps_grad = sums_ref[...] / (2 * OWNERS)
+    new_first = beta_one * first_ref[...] + (1.0 - beta_one) * taps_grad
+    new_second = beta_two * second_ref[...] + (1.0 - beta_two) * taps_grad * taps_grad
+    first_hat = new_first / (1.0 - beta_one**adam_step)
+    second_hat = new_second / (1.0 - beta_two**adam_step)
+    taps_out[...] = taps_ref[...] - learn_rate * first_hat / (jnp.sqrt(second_hat) + adam_eps)
+    first_out[...] = new_first
+    second_out[...] = new_second
+    for onward in leave:
+        onward.wait()
 
 
 def shards(cotangent, gate_values, conv_input, filter_taps, first_moment, second_moment):
@@ -417,8 +446,8 @@
     blocks, summed = pl.pallas_call(
         kernel,
         out_shape=(
-            jax.ShapeDtypeStruct((TOK, LANES, LANES), bf16),
-            jax.ShapeDtypeStruct((LANES, LAGS), f32),
+            jax.ShapeDtypeStruct((1, LANES, width), bf16),
+            jax.ShapeDtypeStruct((LAGS, LANES), f32),
         ),
         in_specs=[hbm, hbm, hbm, vmem, hbm, hbm],
         out_specs=(hbm, vmem),
@@ -458,18 +487,20 @@
             dma((2,)),
         ],
         compiler_params=pltpu.CompilerParams(
-            collective_id=0, has_side_effects=True, vmem_limit_bytes=48 << 20
+            collective_id=0, has_side_effects=True, vmem_limit_bytes=60 << 20
         ),
         name="gated_conv_backward",
-    )(cotangent, gate_values, conv_input, filter_taps, ahead, back)
-    grad_input = jnp.moveaxis(blocks, 0, 1).reshape(LANES, width)
-    taps_grad = summed / lax.axis_size("seq")
-    new_first = beta_one * first_moment + (1.0 - beta_one) * taps_grad
-    new_second = beta_two * second_moment + (1.0 - beta_two) * taps_grad * taps_grad
-    first_hat = new_first / (1.0 - beta_one**adam_step)
-    second_hat = new_second / (1.0 - beta_two**adam_step)
-    new_taps = filter_taps - learn_rate * first_hat / (jnp.sqrt(second_hat) + adam_eps)
-    return (grad_input[None], new_taps, new_first, new_second)
+    )(cotangent, gate_values, conv_input, filter_taps.T, ahead, back)
+    piece = jax.ShapeDtypeStruct((LAGS, LANES), f32)
+    grad_input, new_taps, new_first, new_second = pl.pallas_call(
+        update_kernel,
+        out_shape=(jax.ShapeDtypeStruct((1, LANES, width), bf16), piece, piece, piece),
+        in_specs=[hbm, vmem, vmem, vmem, vmem],
+        out_specs=(hbm, vmem, vmem, vmem),
+        scratch_shapes=[pltpu.VMEM((LANES, width), bf16), dma((PIECES,)), dma((PIECES,))],
+        name="filter_update",
+    )(blocks, summed, filter_taps.T, first_moment.T, second_moment.T)
+    return (grad_input, new_taps.T, new_first.T, new_second.T)
 
 
 def solution(mesh):

time: 69.7 us -> 63.4 us (0.910)
  local copies, waits for them, and re-layouts: 10.3 us -> 0 us
  Pallas kernels: 58.1 us -> 62.4 us
    unnamed x21 -> x0, local copies, waits for them, and re-layouts: 10 us -> none
    pallas_call x1 -> x2, Pallas kernels: 58.1 us -> 62.4 us  [the longest x1 59.1 us: shards(): pl.pallas_call(kernel, out_shape=(jax.ShapeDtypeStruct((1, LANES, width),...]
where the time goes in v1:
time: 63.4 us; the launch traced here: 63 us
  Pallas kernels  62.4 us (98%)
  between operations  0.64 us (1%)
    pallas_call x1, Pallas kernels, shards(): pl.pallas_call(kernel, out_shape=(jax.ShapeDtypeStruct((1, LANES, width),...  59.1 us
    pallas_call x1, Pallas kernels, shards(): pl.pallas_call(update_kernel, out_shape=(jax.ShapeDtypeStruct((1, LANES,...  3.34 us

profile of v1, /device:TPU:1, one launch (start us, length us, event | category | flops | bytes accessed | tf_op | source)
XLA Modules:
  0.0 63.0 jit_solution(11695059209802762414)
XLA Ops:
  0.6 59.1 %gated_conv_backward.1 = (bf16[1,128,2048]{2,1,0:T(8,128)(2,1)}, f32[64,128]{1,0:T(8,128)}) custom-call(bf16[1,128,2048]{2,1,0:T(8,128)(2,1)} %cot_hbm.1, bf16[1,128,2048]{2,1,0:T(8,128)(2,1)} %gate_hbm.1, bf16[1,128,2048]{2,1,0:T(8,128)(2,1)} %input_hbm.1, f32[64,128]{1,0:T(8,128)} %bitcast.6, bf16[2,512,256]{2,1,0:T(8,128)(2,1)} %constant.4.clone.ahead_hbm, ...), custom_call_target="tpu_custom_call" | custom-call | tf_op jit(solution)/shard_map/gated_conv_backward/pallas_call | solution.py:446
  59.7 3.3 %filter_update.1 = (bf16[1,128,2048]{2,1,0:T(8,128)(2,1)}, f32[64,128]{1,0:T(8,128)}, f32[64,128]{1,0:T(8,128)}, f32[64,128]{1,0:T(8,128)}) custom-call(bf16[1,128,2048]{2,1,0:T(8,128)(2,1)} %get-tuple-element.10.grad_ref, f32[64,128]{1,0:T(8,128)} %get-tuple-element.11.sums_ref, f32[64,128]{1,0:T(8,128)} %bitcast.7, f32[64,128]{1,0:T(8,128)} %bitcast.8, ...), custom_call_target="tpu_custom_call" | custom-call | tf_op jit(solution)/shard_map/filter_update/pallas_call | solution.py:495

commit v2 on v1

--- a/solution.py
+++ b/solution.py
@@ -15,7 +15,9 @@
 MESH = pl.DeviceIdType.MESH
 LANES = 128
 TOK = 16
+DEPTH = 8
 OWNERS = 16
+PART = 4
 LAGS = 64
 BLOCK = 256
 PAIRS = 4
@@ -32,20 +34,28 @@
     def split(matrix):
         high = matrix.astype(jnp.bfloat16)
         low = (matrix - high.astype(np.float64)).astype(jnp.bfloat16)
-        return np.stack([high, low])
+        return np.concatenate([high, low], axis=1)
 
     return split(ahead), split(back)
 
 
-def forward(source_ref, spec_ref, ahead_ref):
-    def pair(p, carry):
+def spectrum(ahead_ref, both):
+    return jnp.dot(
+        ahead_ref[...], jnp.concatenate([both, both], axis=0), preferred_element_type=jnp.float32
+    )
+
+
+def forward(source_ref, spec_ref, ahead_ref, first, arrive):
+    def pair(step, carry):
+        p = lax.rem(first - step + PAIRS, PAIRS)
+        arrive(p)
         row = pl.multiple_of(p * (2 * BLOCK), 2 * BLOCK)
-        both = jnp.concatenate(
-            [source_ref[pl.ds(row, BLOCK), :], source_ref[pl.ds(row + BLOCK, BLOCK), :]], axis=1
-        )
-        spec_ref[p] = jnp.dot(
-            ahead_ref[0], both, preferred_element_type=jnp.float32
-        ) + jnp.dot(ahead_ref[1], both, preferred_element_type=jnp.float32)
+        spec_ref[p] = spectrum(
+            ahead_ref,
+            jnp.concatenate(
+                [source_ref[pl.ds(row, BLOCK), :], source_ref[pl.ds(row + BLOCK, BLOCK), :]], axis=1
+            ),
+        )
         return carry
 
     lax.fori_loop(0, PAIRS, pair, 0)
@@ -93,8 +103,8 @@
 
 def backward(spec_ref, back_ref, p):
     both = spec_ref[p].astype(jnp.bfloat16)
-    return jnp.dot(back_ref[0], both, preferred_element_type=jnp.float32) + jnp.dot(
-        back_ref[1], both, preferred_element_type=jnp.float32
+    return jnp.dot(
+        back_ref[...], jnp.concatenate([both, both], axis=0), preferred_element_type=jnp.float32
     )
 
 
@@ -140,10 +150,14 @@
     owner_recv,
     pair_send,
     pair_recv,
+    hello,
 ):
     seq, tok = lax.axis_index("seq"), lax.axis_index("tok")
     core, owner = seq % 2, seq // 2
     sibling = (seq + 1 - 2 * core, tok)
+    depth, side = owner // 2, owner % 2
+    partner = (seq + 2 - 4 * side, tok)
+    above, below = (seq + 4, tok), (seq - 4, tok)
 
     def tok_peer(o):
         return lax.rem(tok + o, TOK)
@@ -170,13 +184,19 @@
 
     def greet(o, carry):
         pl.semaphore_signal(barrier, inc=1, device_id=(seq, tok_peer(o)), device_id_type=MESH)
-        pl.semaphore_signal(
-            barrier, inc=1, device_id=(owner_peer(o) * 2 + core, tok), device_id_type=MESH
-        )
         return carry
 
     lax.fori_loop(1, TOK, greet, 0)
     pl.semaphore_signal(barrier, inc=1, device_id=sibling, device_id_type=MESH)
+    pl.semaphore_signal(barrier, inc=1, device_id=partner, device_id_type=MESH)
+
+    @pl.when(depth > 0)
+    def _():
+        pl.semaphore_signal(barrier, inc=1, device_id=below, device_id_type=MESH)
+
+    @pl.when(depth < DEPTH - 1)
+    def _():
+        pl.semaphore_signal(barrier, inc=1, device_id=above, device_id_type=MESH)
 
     def start_input_load(c, carry):
         input_load(c).start()
@@ -206,7 +226,8 @@
     input_in[my_rows, :] = input_out[tok]
     loads[2].wait()
     loads[3].wait()
-    pl.semaphore_wait(barrier, 2 * (TOK - 1) + 1)
+    neighbours = jnp.minimum(depth, 1) + jnp.minimum(DEPTH - 1 - depth, 1)
+    pl.semaphore_wait(barrier, TOK - 1 + 2 + neighbours)
 
     def scaled_copy(to, frm):
         rows = pl.ds(pl.multiple_of(frm * LANES, LANES), LANES)
@@ -263,8 +284,21 @@
 
     def send_first(o, carry):
         scaled_copy(tok_peer(o), tok).start()
-        taps_copy(owner_peer(o), owner).start()
-        return carry
+        peer = owner_peer(o)
+
+        @pl.when(peer // 2 <= depth)
+        def _():
+            taps_copy(peer, owner).start()
+
+        return carry
+
+    @pl.when(depth > 0)
+    def _():
+        pl.semaphore_wait(hello.at[0], 1)
+
+    @pl.when(depth < DEPTH - 1)
+    def _():
+        pl.semaphore_signal(hello.at[0], inc=1, device_id=above, device_id_type=MESH)
 
     lax.fori_loop(1, TOK, send_first, 0)
 
@@ -273,6 +307,25 @@
         return carry
 
     lax.fori_loop(1, TOK, send_input, 0)
+
+    @pl.when(depth < DEPTH - 1)
+    def _():
+        pl.semaphore_wait(hello.at[1], 1)
+
+    @pl.when(depth > 0)
+    def _():
+        pl.semaphore_signal(hello.at[1], inc=1, device_id=below, device_id_type=MESH)
+
+    def send_above(o, carry):
+        peer = owner_peer(o)
+
+        @pl.when(peer // 2 > depth)
+        def _():
+            taps_copy(peer, owner).start()
+
+        return carry
+
+    lax.fori_loop(1, OWNERS, send_above, 0)
 
     def taps_arrive(o, carry):
         taps_copy(owner, owner_peer(o)).wait_recv()
@@ -292,12 +345,23 @@
 
     taps_pair(core).start()
 
-    def scaled_arrive(o, carry):
-        scaled_copy(tok, tok_peer(o)).wait_recv()
-        return carry
-
-    lax.fori_loop(1, TOK, scaled_arrive, 0)
-    forward(scaled_in, spec_scaled, ahead)
+    def arrivals(copy):
+        def arrive(p):
+            def one(i, carry):
+                peer = p * (TOK // PAIRS) + i
+
+                @pl.when(peer != tok)
+                def _():
+                    copy(tok, peer).wait_recv()
+
+                return carry
+
+            lax.fori_loop(0, TOK // PAIRS, one, 0)
+
+        return arrive
+
+    earliest = lax.rem(tok // (TOK // PAIRS) + PAIRS - 1, PAIRS)
+    forward(scaled_in, spec_scaled, ahead, earliest, arrivals(scaled_copy))
     taps_pair(1 - core).wait_recv()
 
     def taps_forward(p, carry):
@@ -308,9 +372,7 @@
             ],
             axis=1,
         )
-        spec_right[p] = jnp.dot(
-            ahead[0], both, preferred_element_type=jnp.float32
-        ) + jnp.dot(ahead[1], both, preferred_element_type=jnp.float32)
+        spec_right[p] = spectrum(ahead, both)
         return carry
 
     lax.fori_loop(0, PAIRS, taps_forward, 0)
@@ -336,51 +398,57 @@
     own_grad = pltpu.make_async_copy(grad_buf.at[tok], grad_out.at[0, :, my_lanes], local_sem)
     own_grad.start()
 
-    def input_arrive(o, carry):
-        input_copy(tok, tok_peer(o)).wait_recv()
-        return carry
-
-    lax.fori_loop(1, TOK, input_arrive, 0)
-    forward(input_in, spec_right, ahead)
+    forward(input_in, spec_right, ahead, earliest, arrivals(input_copy))
     correlate(spec_scaled, spec_right, spec_prod)
 
-    def sums_back(p, carry):
+    def pair_copy(p):
+        part = pl.ds(p * PART, PART)
+        return pltpu.make_async_remote_copy(
+            src_ref=pair_out.at[part],
+            dst_ref=pair_in.at[part],
+            send_sem=pair_send.at[1 + p],
+            recv_sem=pair_recv.at[1 + p],
+            device_id=sibling,
+            device_id_type=MESH,
+        )
+
+    def rotated(step):
+        return lax.rem(depth // 2 + 1 + step, PAIRS)
+
+    def sums_back(step):
+        p = rotated(step)
         both = backward(spec_prod, back, p)
         for half in range(2):
-            sums[pl.ds(p * 4 + half * 2, 2)] = both[
+            sums[pl.ds(p * PART + half * 2, 2)] = both[
                 :, half * LANES : (half + 1) * LANES
             ].reshape(2, 2, LAGS, LANES)
-        return carry
-
-    lax.fori_loop(0, PAIRS, sums_back, 0)
-
-    def cut(q, carry):
-        pair_out[q] = sums[q, 1 - core].astype(jnp.bfloat16)
-        return carry
-
-    lax.fori_loop(0, OWNERS, cut, 0)
-    pair_copy = pltpu.make_async_remote_copy(
-        src_ref=pair_out,
-        dst_ref=pair_in,
-        send_sem=pair_send.at[1],
-        recv_sem=pair_recv.at[1],
-        device_id=sibling,
-        device_id_type=MESH,
-    )
-    pair_copy.start()
-    pair_copy.wait_recv()
-
-    def join(q, carry):
-        owner_out[q] = (sums[q, core] + pair_in[q].astype(jnp.float32)).astype(jnp.bfloat16)
-        return carry
-
-    lax.fori_loop(0, OWNERS, join, 0)
-
-    def send_owner(o, carry):
-        owner_copy(owner_peer(o), owner).start()
-        return carry
-
-    lax.fori_loop(1, OWNERS, send_owner, 0)
+        for i in range(PART):
+            pair_out[p * PART + i] = sums[p * PART + i, 1 - core].astype(jnp.bfloat16)
+        pair_copy(p).start()
+
+    def sums_join(step):
+        p = rotated(step)
+        pair_copy(p).wait_recv()
+        for i in range(PART):
+            q = p * PART + i
+            owner_out[q] = (sums[q, core] + pair_in[q].astype(jnp.float32)).astype(jnp.bfloat16)
+
+            @pl.when(q != owner)
+            def _():
+                owner_copy(q, owner).start()
+
+    def sums_step(step, carry):
+        @pl.when(step < PAIRS)
+        def _():
+            sums_back(step)
+
+        @pl.when(step > 1)
+        def _():
+            sums_join(step - 2)
+
+        return carry
+
+    lax.fori_loop(0, PAIRS + 2, sums_step, 0)
     owner_in[owner] = owner_out[owner]
 
     def owner_arrive(o, carry):
@@ -404,7 +472,12 @@
 
     lax.fori_loop(1, TOK, finish, 0)
     taps_pair(core).wait_send()
-    pair_copy.wait_send()
+
+    def paired(p, carry):
+        pair_copy(p).wait_send()
+        return carry
+
+    lax.fori_loop(0, PAIRS, paired, 0)
     own_grad.wait()
 
 
@@ -483,8 +556,9 @@
             dma((TOK,)),
             dma((OWNERS,)),
             dma((OWNERS,)),
-            dma((2,)),
-            dma((2,)),
+            dma((1 + PAIRS,)),
+            dma((1 + PAIRS,)),
+            pltpu.SemaphoreType.REGULAR((2,)),
         ],
         compiler_params=pltpu.CompilerParams(
             collective_id=0, has_side_effects=True, vmem_limit_bytes=60 << 20

time: 63.4 us -> 62.5 us (0.986)
  Pallas kernels: 62.4 us -> 61.5 us
    pallas_call x1, Pallas kernels: 59.1 us -> 58.2 us  [shards(): pl.pallas_call(kernel, out_shape=(jax.ShapeDtypeStruct((1, LANES, width),...]
where the time goes in v2:
time: 62.5 us; the launch traced here: 62.2 us
  Pallas kernels  61.5 us (98%)
  between operations  0.64 us (1%)
    pallas_call x1, Pallas kernels, shards(): pl.pallas_call(kernel, out_shape=(jax.ShapeDtypeStruct((1, LANES, width),...  58.2 us
    pallas_call x1, Pallas kernels, shards(): pl.pallas_call(update_kernel, out_shape=(jax.ShapeDtypeStruct((1, LANES,...  3.34 us

profile of v2, /device:TPU:1, one launch (start us, length us, event | category | flops | bytes accessed | tf_op | source)
XLA Modules:
  0.0 62.2 jit_solution(1546794396682976243)
XLA Ops:
  0.6 58.2 %gated_conv_backward.1 = (bf16[1,128,2048]{2,1,0:T(8,128)(2,1)}, f32[64,128]{1,0:T(8,128)}) custom-call(bf16[1,128,2048]{2,1,0:T(8,128)(2,1)} %cot_hbm.1, bf16[1,128,2048]{2,1,0:T(8,128)(2,1)} %gate_hbm.1, bf16[1,128,2048]{2,1,0:T(8,128)(2,1)} %input_hbm.1, f32[64,128]{1,0:T(8,128)} %bitcast.6, bf16[512,512]{1,0:T(8,128)(2,1)} %constant.4.clone.ahead_hbm, ...), custom_call_target="tpu_custom_call" | custom-call | tf_op jit(solution)/shard_map/gated_conv_backward/pallas_call | solution.py:519
  58.8 3.3 %filter_update.1 = (bf16[1,128,2048]{2,1,0:T(8,128)(2,1)}, f32[64,128]{1,0:T(8,128)}, f32[64,128]{1,0:T(8,128)}, f32[64,128]{1,0:T(8,128)}) custom-call(bf16[1,128,2048]{2,1,0:T(8,128)(2,1)} %get-tuple-element.10.grad_ref, f32[64,128]{1,0:T(8,128)} %get-tuple-element.11.sums_ref, f32[64,128]{1,0:T(8,128)} %bitcast.7, f32[64,128]{1,0:T(8,128)} %bitcast.8, ...), custom_call_target="tpu_custom_call" | custom-call | tf_op jit(solution)/shard_map/filter_update/pallas_call | solution.py:569

commit v3 on v2

--- a/solution.py
+++ b/solution.py
@@ -306,7 +306,6 @@
         input_copy(tok_peer(o), tok).start()
         return carry
 
-    lax.fori_loop(1, TOK, send_input, 0)
 
     @pl.when(depth < DEPTH - 1)
     def _():
@@ -326,6 +325,7 @@
         return carry
 
     lax.fori_loop(1, OWNERS, send_above, 0)
+    lax.fori_loop(1, TOK, send_input, 0)
 
     def taps_arrive(o, carry):
         taps_copy(owner, owner_peer(o)).wait_recv()
@@ -482,29 +482,43 @@
 
 
 def update_kernel(
-    grad_ref, sums_ref, taps_ref, first_ref, second_ref, grad_out, taps_out, first_out, second_out, held, in_sem, out_sem
+    grad_ref, sums_ref, taps_ref, first_ref, second_ref,
+    grad_out, taps_out, first_out, second_out,
+    held, small, done, in_sem, out_sem, small_sem, done_sem,
 ):
     rows = LANES // PIECES
+    smalls = [
+        pltpu.make_async_copy(ref, small.at[i], small_sem.at[i])
+        for i, ref in enumerate((sums_ref, taps_ref, first_ref, second_ref))
+    ]
     arrive, leave = [], []
     for i in range(PIECES):
         piece = pl.ds(i * rows, rows)
         arrive.append(pltpu.make_async_copy(grad_ref.at[0, piece], held.at[piece], in_sem.at[i]))
         leave.append(pltpu.make_async_copy(held.at[piece], grad_out.at[0, piece], out_sem.at[i]))
-    for copy in arrive:
+    for copy in smalls + arrive:
+        copy.start()
+    for copy in smalls:
+        copy.wait()
+    taps_grad = small[0] / (2 * OWNERS)
+    new_first = beta_one * small[2] + (1.0 - beta_one) * taps_grad
+    new_second = beta_two * small[3] + (1.0 - beta_two) * taps_grad * taps_grad
+    first_hat = new_first / (1.0 - beta_one**adam_step)
+    second_hat = new_second / (1.0 - beta_two**adam_step)
+    done[0] = small[1] - learn_rate * first_hat / (jnp.sqrt(second_hat) + adam_eps)
+    done[1] = new_first
+    done[2] = new_second
+    finished = [
+        pltpu.make_async_copy(done.at[i], ref, done_sem.at[i])
+        for i, ref in enumerate((taps_out, first_out, second_out))
+    ]
+    for copy in finished:
         copy.start()
     for copy, onward in zip(arrive, leave):
         copy.wait()
         onward.start()
-    taps_grad = sums_ref[...] / (2 * OWNERS)
-    new_first = beta_one * first_ref[...] + (1.0 - beta_one) * taps_grad
-    new_second = beta_two * second_ref[...] + (1.0 - beta_two) * taps_grad * taps_grad
-    first_hat = new_first / (1.0 - beta_one**adam_step)
-    second_hat = new_second / (1.0 - beta_two**adam_step)
-    taps_out[...] = taps_ref[...] - learn_rate * first_hat / (jnp.sqrt(second_hat) + adam_eps)
-    first_out[...] = new_first
-    second_out[...] = new_second
-    for onward in leave:
-        onward.wait()
+    for copy in finished + leave:
+        copy.wait()
 
 
 def shards(cotangent, gate_values, conv_input, filter_taps, first_moment, second_moment):
@@ -569,9 +583,18 @@
     grad_input, new_taps, new_first, new_second = pl.pallas_call(
         update_kernel,
         out_shape=(jax.ShapeDtypeStruct((1, LANES, width), bf16), piece, piece, piece),
-        in_specs=[hbm, vmem, vmem, vmem, vmem],
-        out_specs=(hbm, vmem, vmem, vmem),
-        scratch_shapes=[pltpu.VMEM((LANES, width), bf16), dma((PIECES,)), dma((PIECES,))],
+        in_specs=[hbm] * 5,
+        out_specs=(hbm,) * 4,
+        scratch_shapes=[
+            pltpu.VMEM((LANES, width), bf16),
+            pltpu.VMEM((4, LAGS, LANES), f32),
+            pltpu.VMEM((3, LAGS, LANES), f32),
+            dma((PIECES,)),
+            dma((PIECES,)),
+            dma((4,)),
+            dma((3,)),
+        ],
+        compiler_params=pltpu.CompilerParams(vmem_limit_bytes=60 << 20),
         name="filter_update",
     )(blocks, summed, filter_taps.T, first_moment.T, second_moment.T)
     return (grad_input, new_taps.T, new_first.T, new_second.T)

time: 62.5 us -> 61.3 us (0.981)
  Pallas kernels: 61.5 us -> 60.3 us
    pallas_call x1, Pallas kernels: 3.34 us -> 2.22 us  [shards(): pl.pallas_call(update_kernel, out_shape=(jax.ShapeDtypeStruct((1, LANES,...]
where the time goes in v3:
time: 61.3 us; the launch traced here: 61 us
  Pallas kernels  60.3 us (98%)
  between operations  0.64 us (1%)
    pallas_call x1, Pallas kernels, shards(): pl.pallas_call(kernel, out_shape=(jax.ShapeDtypeStruct((1, LANES, width),...  58.1 us
    pallas_call x1, Pallas kernels, shards(): pl.pallas_call(update_kernel, out_shape=(jax.ShapeDtypeStruct((1, LANES,...  2.22 us

profile of v3, /device:TPU:1, one launch (start us, length us, event | category | flops | bytes accessed | tf_op | source)
XLA Modules:
  0.0 61.0 jit_solution(5547481000744824387)
XLA Ops:
  0.6 58.1 %gated_conv_backward.1 = (bf16[1,128,2048]{2,1,0:T(8,128)(2,1)}, f32[64,128]{1,0:T(8,128)}) custom-call(bf16[1,128,2048]{2,1,0:T(8,128)(2,1)} %cot_hbm.1, bf16[1,128,2048]{2,1,0:T(8,128)(2,1)} %gate_hbm.1, bf16[1,128,2048]{2,1,0:T(8,128)(2,1)} %input_hbm.1, f32[64,128]{1,0:T(8,128)} %bitcast.6, bf16[512,512]{1,0:T(8,128)(2,1)} %constant.4.clone.ahead_hbm, ...), custom_call_target="tpu_custom_call" | custom-call | tf_op jit(solution)/shard_map/gated_conv_backward/pallas_call | solution.py:533
  58.7 2.2 %filter_update.1 = (bf16[1,128,2048]{2,1,0:T(8,128)(2,1)}, f32[64,128]{1,0:T(8,128)}, f32[64,128]{1,0:T(8,128)}, f32[64,128]{1,0:T(8,128)}) custom-call(bf16[1,128,2048]{2,1,0:T(8,128)(2,1)} %get-tuple-element.10.grad_ref, f32[64,128]{1,0:T(8,128)} %get-tuple-element.11.sums_ref, f32[64,128]{1,0:T(8,128)} %bitcast.7, f32[64,128]{1,0:T(8,128)} %bitcast.8, ...), custom_call_target="tpu_custom_call" | custom-call | tf_op jit(solution)/shard_map/filter_update/pallas_call | solution.py:583
